TPU v7x, 32 devices: a whole 2x2x4 slice. The times are simulated.
32 devices in a mesh: sweep: 2 (over x), cell: 8 (over z, y), head: 2 (over core).
Axes of the slice: x: 2, y: 2, z: 4, core: 2. Of those that a mesh axis runs over, the one named last changes fastest.
Arguments:
- hidden: bfloat16 [4096, 8192], P(('sweep', 'cell'), 'head'), parts along dimension 0, may hold values from -6 to 6
- w_key: bfloat16 [8192, 512], P(None, 'head'), may hold values from -0.0625 to 0.0625
- w_value: bfloat16 [8192, 512], P(None, 'head'), may hold values from -0.0625 to 0.0625
- queries: bfloat16 [4096, 4096], P(('sweep', 'cell'), 'head'), parts along dimension 0, as said below
- span_order: int32 [16, 8], P(('sweep', 'cell')), parts along dimension 0, may hold values from 0 to 7, as said below
- span_count: int32 [16], P(('sweep', 'cell')), parts along dimension 0, may hold values from 2 to 8
- needle: int32 [16], P(('sweep', 'cell')), parts along dimension 0, may hold values from 0 to 7, as said below
- owners: int32 [8, 2], P('sweep'), parts along dimension 0, may hold values from 0 to 7, as said below
Outputs:
- attended: bfloat16 [4096, 4096], P(('sweep', 'cell'), 'head'), parts along dimension 0
There are 2 independent parts, one for each index of `sweep`. A program takes and returns all parts, laid end to end along the dimension named above; an argument that names none is the same for every part. Nothing has to cross between parts.
Inputs may be any that keep to these rules, and one draw needn't show every extreme that they name: `span_order`: every row is a permutation of 0 to 7. `needle`: below the same cell's span_count. `owners`: all 8 entries of a part are distinct. `queries`: every entry lies in -64 to 64.
All inputs are finite; a program needn't handle non-finite values.
Results may differ from a plain program's by a relative error of at most 0.004.
The roundings to bfloat16 on the way count: a program that leaves them out, or rounds other values in their place, can miss the bound.
Values may be sent and summed in bfloat16 or wider, within the bound.
A program may use at most 128 MiB of HBM per device.

v0:
```python
import math

import jax
import jax.numpy as jnp
from jax import lax
from jax.sharding import PartitionSpec as P

HD = 128
ROUNDS = 4
GROUP = 8


rope_theta = 500000.0


def rotary(values, positions):
    half_dim = values.shape[-1] // 2
    frequency = rope_theta ** (-2.0 * jnp.arange(half_dim, dtype=jnp.float32) / values.shape[-1])
    angles = positions.astype(jnp.float32)[..., None] * frequency
    cosine = jnp.cos(angles)
    sine_part = jnp.sin(angles)
    first = values[..., :half_dim]
    second = values[..., half_dim:]
    return jnp.concatenate(
        [first * cosine - second * sine_part, second * cosine + first * sine_part], axis=-1
    )


def on_device(hidden, w_key, w_value, queries, span_order, span_count, needle, owners):
    span_rows = hidden.shape[0]
    local_heads = w_key.shape[1] // HD
    score_scale = 1.0 / math.sqrt(HD)
    hidden_piece = lax.all_gather(hidden, "head", axis=1, tiled=True)
    key_sum = jnp.dot(hidden_piece, w_key, preferred_element_type=jnp.float32)
    value_sum = jnp.dot(hidden_piece, w_value, preferred_element_type=jnp.float32)
    own_span = jnp.stack([key_sum.astype(jnp.bfloat16), value_sum.astype(jnp.bfloat16)])
    cell_order = span_order[0]
    cell_count = span_count[0]
    needle_slot = needle[0]
    needle_place = cell_order[needle_slot]
    lane_ids = jnp.arange(span_rows, dtype=jnp.int32)
    query_pos = needle_place * span_rows + lane_ids
    rot_query = rotary(
        queries.reshape(span_rows, local_heads, GROUP, HD).astype(jnp.float32),
        query_pos[:, None, None],
    ).astype(jnp.bfloat16)
    carried = (
        jnp.full((span_rows, local_heads, GROUP), -1e30, jnp.float32),
        jnp.zeros((span_rows, local_heads, GROUP), jnp.float32),
        jnp.zeros((span_rows, local_heads, GROUP, HD), jnp.float32),
    )
    every_span = lax.all_gather(own_span[None], "cell", axis=0, tiled=True)
    for round_index in range(ROUNDS):
        pair_kv = every_span[owners[round_index]]
        attend_running_max, attend_weight_sum, attend_accumulated = carried
        slot_ids = 2 * round_index + jnp.arange(2, dtype=jnp.int32)
        slot_places = cell_order[slot_ids]
        key_pos = slot_places[:, None] * span_rows + lane_ids[None, :]
        rot_keys = rotary(
            pair_kv[:, 0].reshape(2, span_rows, local_heads, HD).astype(jnp.float32),
            key_pos[:, :, None],
        )
        rot_keys = rot_keys.astype(jnp.bfloat16).reshape(2 * span_rows, local_heads, HD)
        pair_values = pair_kv[:, 1].reshape(2 * span_rows, local_heads, HD)
        scores = (
            jnp.einsum("ikgd,jkd->ikgj", rot_query, rot_keys, preferred_element_type=jnp.float32)
            * score_scale
        )
        before = (slot_ids < cell_count) & (slot_places < needle_place)
        causal = (slot_ids == needle_slot)[:, None, None] & (
            lane_ids[None, None, :] <= lane_ids[None, :, None]
        )
        visible = jnp.transpose(before[:, None, None] | causal, (1, 0, 2)).reshape(
            span_rows, 2 * span_rows
        )
        scores = jnp.where(visible[:, None, None, :], scores, -jnp.inf)
        new_max = jnp.maximum(attend_running_max, jnp.max(scores, axis=-1))
        rescale = jnp.exp(attend_running_max - new_max)
        weights = jnp.exp(scores - new_max[..., None])
        attend_weight_sum = attend_weight_sum * rescale + jnp.sum(weights, axis=-1)
        attend_accumulated = attend_accumulated * rescale[..., None] + jnp.einsum(
            "ikgj,jkd->ikgd",
            weights.astype(jnp.bfloat16),
            pair_values,
            preferred_element_type=jnp.float32,
        )
        carried = (new_max, attend_weight_sum, attend_accumulated)
    running_max, weight_sum, accumulated = carried
    mixed_rows = accumulated / weight_sum[..., None]
    return mixed_rows.astype(jnp.bfloat16).reshape(span_rows, local_heads * GROUP * HD)


def solution(mesh):
    in_specs = (
        P(("sweep", "cell"), "head"),
        P(None, "head"),
        P(None, "head"),
        P(("sweep", "cell"), "head"),
        P(("sweep", "cell"), None),
        P(("sweep", "cell")),
        P(("sweep", "cell")),
        P("sweep", None),
    )
    out_specs = P(("sweep", "cell"), "head")
    return jax.shard_map(
        on_device, mesh=mesh, in_specs=in_specs, out_specs=out_specs, check_vma=False
    )
```

profile of v0, /device:TPU:0, one launch (start us, length us, event | category | flops | bytes accessed | tf_op | source)
XLA Modules:
  0.0 158.6 jit_solution(3886008486480580609)
XLA Ops:
  6.5 0.7 all-gather.4.cloned.1.call-update
  11.5 0.7 compare_and_fusion.2
  13.7 0.7 compare_and_fusion
  14.5 1.5 copy.57
  16.0 1.2 fusion.78
  17.2 2.0 %copy.103 = f32[256,2,8,64]{3,0,2,1:T(8,128)S(1)} copy(f32[256,2,8,64]{0,3,2,1:T(8,128)} %get-tuple-element.18) | data formatting | bytes 2097152
  19.2 1.9 %copy.102 = f32[256,2,8,64]{3,0,2,1:T(8,128)} copy(f32[256,2,8,64]{0,3,2,1:T(8,128)S(1)} %get-tuple-element.19) | data formatting | bytes 2097152
  21.1 4.2 %all-gather.4.cloned.1.call-done = bf16[256,8192]{1,0:T(8,128)(2,1)} async-done(((bf16[256,4096]{1,0:T(8,128)(2,1)}), bf16[256,8192]{1,0:T(8,128)(2,1)}) %all-gather.4.cloned.1.call-update) | async-done | bytes 4194320 | tf_op jit(solution)/shard_map/all_gather | solution.py:33
  25.3 4.8 %fusion.32 = bf16[1,256,256]{2,1,0:T(8,128)(2,1)S(1)} fusion(bf16[256,8192]{1,0:T(8,128)(2,1)} %all-gather.4.cloned.1.call-done, bf16[8192,256]{1,0:T(8,128)(2,1)} %param.10), kind=kOutput, calls=%fused_computation.54 | convolution fusion | flops 1073807360 | bytes 8519680 | tf_op jit(solution)/shard_map/dot_general | solution.py:35
  30.2 1.1 copy-done.8
  31.2 1.2 fusion.31
  32.5 0.7 pad_maximum_fusion.1
  33.3 0.8 fusion.33
  34.9 2.4 %subtract_convert_fusion = (bf16[256,2,8,64]{3,0,2,1:T(8,128)(2,1)S(1)}, bf16[256,2,8,64]{3,0,2,1:T(8,128)(2,1)S(1)}) fusion(f32[256,2,8,64]{3,0,2,1:T(8,128)S(1)} %copy.103, f32[256,2,8,64]{3,0,2,1:T(8,128)} %copy.102, f32[256,64]{1,0:T(8,128)S(1)} %get-tuple-element.51, f32[256,64]{1,0:T(8,128)S(1)} %get-tuple-element.50), kind=kLoop, calls=%fused_computation.46 | loop fusion | flops 2097152 | bytes 3276800 | tf_op jit(solution)/shard_map/convert.17
  38.1 2.8 %multiply_cosine_fusion.4 = (f32[2,256,64]{1,2,0:T(8,128)S(1)}, f32[2,256,64]{1,2,0:T(8,128)}, f32[2,256,64]{1,2,0:T(8,128)}, f32[2,256,64]{1,2,0:T(8,128)}, f32...) fusion(f32[64]{0:T(128)S(1)} %multiply_power_fusion, ...), kind=kLoop, calls=%fused_computation.103 | loop fusion | flops 131072 | bytes 1057024 | tf_op jit(solution)/shard_map/cos | solution.py:20
  40.9 43.0 %all-gather.6.cloned.1.call-done = bf16[16,256,256]{2,1,0:T(8,128)(2,1)} async-done(((bf16[2,256,256]{2,1,0:T(8,128)(2,1)}), bf16[16,256,256]{2,1,0:T(8,128)(2,1)}) %all-gather.6.cloned.1.call-update) | async-done | bytes 2097168 | tf_op jit(solution)/shard_map/all_gather | solution.py:52
  83.8 2.2 %gather_fusion.7 = bf16[2,2,256,256]{3,2,1,0:T(8,128)(2,1)S(1)} fusion(bf16[8,2,256,256]{3,2,1,0:T(8,128)(2,1)} %bitcast.185, s32[1024]{0:T(1024)S(1)} %pad_clamp_fusion), kind=kCustom, calls=%fused_computation.7 | custom fusion | bytes 1048584 | tf_op jit(solution)/shard_map/gather | solution.py:54
  86.1 0.8 reshape.735
  86.9 2.2 %gather_fusion.5 = bf16[2,2,256,256]{3,2,1,0:T(8,128)(2,1)S(1)} fusion(bf16[8,2,256,256]{3,2,1,0:T(8,128)(2,1)} %bitcast.186, s32[1024]{0:T(1024)S(1)} %pad_clamp_fusion.2), kind=kCustom, calls=%fused_computation.5 | custom fusion | bytes 1048584 | tf_op jit(solution)/shard_map/gather | solution.py:54
  89.1 0.8 reshape.734
  89.9 3.0 %gather_fusion.3 = bf16[2,2,256,256]{3,2,1,0:T(8,128)(2,1)} fusion(bf16[8,2,256,256]{3,2,1,0:T(8,128)(2,1)} %bitcast.187, s32[1024]{0:T(1024)S(1)} %pad_clamp_fusion.4), kind=kCustom, calls=%fused_computation.3 | custom fusion | bytes 1048584 | tf_op jit(solution)/shard_map/gather | solution.py:54
  92.9 3.0 %gather_fusion.1 = bf16[2,2,256,256]{3,2,1,0:T(8,128)(2,1)} fusion(bf16[8,2,256,256]{3,2,1,0:T(8,128)(2,1)} %bitcast.188, s32[1024]{0:T(1024)S(1)} %pad_clamp_fusion.6), kind=kCustom, calls=%fused_computation.1 | custom fusion | bytes 1048584 | tf_op jit(solution)/shard_map/gather | solution.py:54
  95.8 1.1 fusion.79
  96.9 0.8 reshape.732
  97.7 1.9 %fusion.80 = (bf16[2,1,256,256]{3,2,1,0:T(8,128)(2,1)S(1)}, f32[2,1,256,256]{3,2,1,0:T(8,128)}) fusion(bf16[2,2,256,256]{3,2,1,0:T(8,128)(2,1)} %gather_fusion.3), kind=kLoop, calls=%fused_computation.180 | loop fusion | flops 131072 | bytes 1310720 | tf_op jit(solution)/shard_map/slice | solution.py:64
  99.6 0.8 reshape.733
  100.4 2.0 %copy.62 = f32[2,1,256,256]{2,3,0,1:T(8,128)} copy(f32[2,1,256,256]{3,2,1,0:T(8,128)} %get-tuple-element.31) | data formatting | bytes 1048576 | tf_op jit(solution)/shard_map/convert_element_type | solution.py:60
  102.4 1.0 copy.54
  103.8 1.2 subtract_convert_fusion.4
  105.1 1.2 subtract_convert_fusion.3
  106.5 1.7 %subtract_convert_fusion.2 = (bf16[2,256,2,64]{1,3,2,0:T(8,128)(2,1)}, bf16[2,256,2,64]{1,3,2,0:T(8,128)(2,1)S(1)}) fusion(f32[2,256,2,128]{1,3,2,0:T(8,128)S(1)} %bitcast.182, f32[2,256,64]{1,2,0:T(8,128)} %get-tuple-element.54, f32[2,256,64]{1,2,0:T(8,128)} %get-tuple-element.55), kind=kLoop, calls=%fused_computation.88 | loop fusion | flops 524288 | bytes 1048576 | tf_op jit(solution)/shard_map/convert.12
  108.2 1.1 copy.68
  109.3 1.8 %subtract_convert_fusion.1 = (bf16[2,256,2,64]{1,3,2,0:T(8,128)(2,1)}, bf16[2,256,2,64]{1,3,2,0:T(8,128)(2,1)}) fusion(f32[2,256,2,128]{1,3,2,0:T(8,128)S(1)} %bitcast.181, f32[2,256,64]{1,2,0:T(8,128)} %get-tuple-element.56, f32[2,256,64]{1,2,0:T(8,128)} %get-tuple-element.57), kind=kLoop, calls=%fused_computation.86 | loop fusion | flops 524288 | bytes 1048576 | tf_op jit(solution)/shard_map/convert.8
  111.1 1.1 copy.73
  112.7 1.7 %copy.74 = bf16[2,256,2,64]{3,1,0,2:T(8,128)(2,1)} copy(bf16[2,256,2,64]{1,3,2,0:T(8,128)(2,1)} %get-tuple-element.27) | data formatting | bytes 262144 | tf_op jit(solution)/shard_map/convert.7
  114.4 5.6 %fusion.11 = (f32[256,2,8]{0,2,1:T(8,128)S(1)}, f32[2,512,256,8]{2,1,3,0:T(8,128)}) fusion(pred[256,512]{0,1:T(8,128)(4,1)S(1)} %get-tuple-element.37, bf16[256,2,8,128]{3,0,2,1:T(8,128)(2,1)S(1)} %pad_maximum_fusion, bf16[512,2,64]{2,0,1:T(8,128)(2,1)} %bitcast.196, bf16[512,2,64]{2,0,1:T(8,128)(2,1)S(1)} %bitcast.194), kind=kOutput, calls=%fused_computation.27 | convolution fusion | flops 543682560 | bytes 9846784 | tf_op jit(solution)/shard_map/ikgd,jkd->ikgj/dot_general | solution.py:66
  120.0 1.4 fusion.10
  121.5 1.4 fusion.9
  122.9 1.4 fusion.8
  124.4 5.2 %fusion.6 = f32[256,2,8]{0,2,1:T(8,128)S(1)} fusion(f32[2,512,256,8]{2,1,3,0:T(8,128)} %get-tuple-element.59, f32[256,2,8]{0,2,1:T(8,128)S(1)} %get-tuple-element.13, pred[256,512]{0,1:T(8,128)(4,1)S(1)} %get-tuple-element.37), kind=kLoop, calls=%fused_computation.22 | loop fusion | flops 8384512 | bytes 8552448 | tf_op jit(solution)/shard_map/reduce_sum | solution.py:80
  129.6 6.9 %fusion.12 = f32[2,128,256,8]{2,1,3,0:T(8,128)} fusion(f32[2,512,256,8]{2,1,3,0:T(8,128)} %get-tuple-element.59, f32[256,2,8]{0,2,1:T(8,128)S(1)} %get-tuple-element.13, pred[256,512]{0,1:T(8,128)(4,1)S(1)} %get-tuple-element.37, bf16[512,2,128,1]{2,1,0,3:T(2,128)(2,1)S(1)} %bitcast.199), kind=kOutput, calls=%fused_computation.28 | convolution fusion | flops 545259520 | bytes 10895360 | tf_op jit(solution)/shard_map/ikgj,jkd->ikgd/dot_general | solution.py:81
  136.5 1.9 %fusion.4 = f32[256,2,8]{0,2,1:T(8,128)S(1)} fusion(f32[2,512,256,8]{2,1,3,0:T(8,128)S(1)} %get-tuple-element.61, f32[256,2,8]{0,2,1:T(8,128)S(1)} %get-tuple-element.14, pred[256,512]{0,1:T(8,128)(4,1)S(1)} %get-tuple-element.38), kind=kLoop, calls=%fused_computation.20 | loop fusion | flops 8384512 | bytes 8552448 | tf_op jit(solution)/shard_map/reduce_sum | solution.py:80
  138.4 3.5 %fusion.14 = f32[2,128,256,8]{2,1,3,0:T(8,128)} fusion(f32[2,512,256,8]{2,1,3,0:T(8,128)S(1)} %get-tuple-element.61, f32[256,2,8]{0,2,1:T(8,128)S(1)} %get-tuple-element.14, pred[256,512]{0,1:T(8,128)(4,1)S(1)} %get-tuple-element.38, bf16[512,2,128,1]{2,1,0,3:T(2,128)(2,1)S(1)} %bitcast.200), kind=kOutput, calls=%fused_computation.29 | convolution fusion | flops 545259520 | bytes 10895360 | tf_op jit(solution)/shard_map/ikgj,jkd->ikgd/dot_general | solution.py:81
  141.9 1.7 %fusion.2 = f32[256,2,8]{0,2,1:T(8,128)S(1)} fusion(f32[2,512,256,8]{2,1,3,0:T(8,128)S(1)} %get-tuple-element.63, f32[256,2,8]{0,2,1:T(8,128)S(1)} %get-tuple-element.15, pred[256,512]{0,1:T(8,128)(4,1)S(1)} %get-tuple-element.39), kind=kLoop, calls=%fused_computation.18 | loop fusion | flops 8384512 | bytes 8552448 | tf_op jit(solution)/shard_map/reduce_sum | solution.py:80
  143.6 2.1 %fusion.16 = f32[2,128,256,8]{2,1,3,0:T(8,128)S(1)} fusion(f32[2,512,256,8]{2,1,3,0:T(8,128)S(1)} %get-tuple-element.63, f32[256,2,8]{0,2,1:T(8,128)S(1)} %get-tuple-element.15, pred[256,512]{0,1:T(8,128)(4,1)S(1)} %get-tuple-element.39, bf16[512,2,128,1]{2,1,0,3:T(2,128)(2,1)S(1)} %bitcast.201), kind=kOutput, calls=%fused_computation.30 | convolution fusion | flops 545259520 | bytes 10895360 | tf_op jit(solution)/shard_map/ikgj,jkd->ikgd/dot_general | solution.py:81
  145.8 1.7 %fusion = f32[256,2,8]{0,2,1:T(8,128)S(1)} fusion(f32[2,512,256,8]{2,1,3,0:T(8,128)S(1)} %get-tuple-element.65, f32[256,2,8]{0,2,1:T(8,128)S(1)} %get-tuple-element.41, pred[256,512]{0,1:T(8,128)(4,1)S(1)} %get-tuple-element.36), kind=kLoop, calls=%fused_computation.16 | loop fusion | flops 8384512 | bytes 8552448 | tf_op jit(solution)/shard_map/reduce_sum | solution.py:80
  147.6 2.8 %fusion.25 = bf16[256,2,8,128]{0,3,2,1:T(8,128)(2,1)S(1)} fusion(f32[2,128,256,8]{2,1,3,0:T(8,128)S(1)} %copy-done.9, f32[2,128,256,8]{2,1,3,0:T(8,128)S(1)} %copy-done.10, f32[2,128,256,8]{2,1,3,0:T(8,128)S(1)} %fusion.16, f32[2,512,256,8]{2,1,3,0:T(8,128)S(1)} %get-tuple-element.65, f32[256,2,8]{0,2,1:T(8,128)S(1)} %get-tuple-element.41, ...), kind=kOutput, calls=%fused_computation.38 | convolution fusion | flops 549978112 | bytes 16220160 | tf_op jit(solution)/shard_map/ikgj,jkd->ikgd/dot_general | solution.py:81
  150.3 1.4 copy.77
  (84 shorter events, 7.0 us)
Async XLA Ops:
  6.5 2.5 %copy-start = (s32[1,8]{1,0:T(1,128)S(1)}, s32[1,8]{1,0:T(1,128)}, u32[]{:S(2)}) copy-start(s32[1,8]{1,0:T(1,128)} %param.12) | copy-start | bytes 100
  6.5 18.8 %all-gather.4.cloned.1.call-start = ((), (), s32[]{:S(2)}) async-start(), calls=%async_computation | async-start | bytes 6291456 | tf_op jit(solution)/shard_map/all_gather | solution.py:33
  7.3 76.6 %all-gather.6.cloned.1.call-start = ((), (), s32[]{:S(2)}) async-start(), calls=%async_computation.1 | async-start | bytes 2359296 | tf_op jit(solution)/shard_map/all_gather | solution.py:52
  25.3 4.9 %copy-start.7 = (bf16[8192,256]{1,0:T(8,128)(2,1)S(1)}, bf16[8192,256]{1,0:T(8,128)(2,1)}, u32[]{:S(2)}) copy-start(bf16[8192,256]{1,0:T(8,128)(2,1)} %param.9) | copy-start | bytes 12582916
  25.3 5.9 %copy-start.8 = (bf16[256,8192]{1,0:T(8,128)(2,1)S(1)}, bf16[256,8192]{1,0:T(8,128)(2,1)}, u32[]{:S(2)}) copy-start(bf16[256,8192]{1,0:T(8,128)(2,1)} %all-gather.4.cloned.1.call-done) | copy-start | bytes 12582916
  31.2 2.8 %copy-start.6 = (s32[4,2]{0,1:T(2,128)S(1)}, s32[4,2]{0,1:T(2,128)}, u32[]{:S(2)}) copy-start(s32[4,2]{0,1:T(2,128)} %param.15) | copy-start | bytes 100
  122.9 6.6 %copy-start.3 = (bf16[512,2,128]{2,1,0:T(2,128)(2,1)S(1)}, bf16[512,2,128]{2,1,0:T(2,128)(2,1)}, u32[]{:S(2)}) copy-start(bf16[512,2,128]{2,1,0:T(2,128)(2,1)} %reshape.735) | copy-start | bytes 786436
  129.6 8.8 %copy-start.4 = (bf16[512,2,128]{2,1,0:T(2,128)(2,1)S(1)}, bf16[512,2,128]{2,1,0:T(2,128)(2,1)}, u32[]{:S(2)}) copy-start(bf16[512,2,128]{2,1,0:T(2,128)(2,1)} %reshape.734) | copy-start | bytes 786436
  138.4 5.2 %copy-start.5 = (bf16[512,2,128]{2,1,0:T(2,128)(2,1)S(1)}, bf16[512,2,128]{2,1,0:T(2,128)(2,1)}, u32[]{:S(2)}) copy-start(bf16[512,2,128]{2,1,0:T(2,128)(2,1)} %reshape.733) | copy-start | bytes 786436
  143.6 3.9 %copy-start.2 = (bf16[512,2,128]{2,1,0:T(2,128)(2,1)S(1)}, bf16[512,2,128]{2,1,0:T(2,128)(2,1)}, u32[]{:S(2)}) copy-start(bf16[512,2,128]{2,1,0:T(2,128)(2,1)} %reshape.732) | copy-start | bytes 786436
  143.6 3.9 %copy-start.9 = (f32[2,128,256,8]{2,1,3,0:T(8,128)S(1)}, f32[2,128,256,8]{2,1,3,0:T(8,128)}, u32[]{:S(2)}) copy-start(f32[2,128,256,8]{2,1,3,0:T(8,128)} %fusion.12) | copy-start | bytes 6291460
  143.6 3.9 %copy-start.10 = (f32[2,128,256,8]{2,1,3,0:T(8,128)S(1)}, f32[2,128,256,8]{2,1,3,0:T(8,128)}, u32[]{:S(2)}) copy-start(f32[2,128,256,8]{2,1,3,0:T(8,128)} %fusion.14) | copy-start | bytes 6291460
  147.5 4.2 %copy-start.1 = (s32[1,8]{1,0:T(1,128)S(1)}, s32[1,8]{1,0:T(1,128)}, u32[]{:S(2)}) copy-start(s32[1,8]{1,0:T(1,128)} %param.12) | copy-start | bytes 100
Sparse Core Ops, SparseCore 0:
  8.9 16.3 all-gather.3
  33.4 50.4 all-gather.5
where the time goes:
time: 159 us
  waiting for transfers between devices  47.9 us (30%)
  local copies, waits for them, and re-layouts  34.8 us (22%)
  matrix products  31.3 us (20%)
  other arithmetic  28.9 us (18%)
  between operations  15.8 us (10%)
    all_gather x1, waiting for transfers between devices, on_device(): every_span = lax.all_gather(own_span[None], 'cell', axis=0, tiled=True)  43 us
    dot_general x4, matrix products, on_device(): jnp.einsum('ikgj,jkd->ikgd', weights.astype(jnp.bfloat16), pair_values, p...  15.3 us
    reduce_sum x4, other arithmetic, on_device(): attend_weight_sum = attend_weight_sum * rescale + jnp.sum(weights, axis=-1)  10.5 us
    gather x4, local copies, waits for them, and re-layouts, on_device(): pair_kv = every_span[owners[round_index]]  10.3 us
    dot_general x4, matrix products, on_device(): jnp.einsum('ikgd,jkd->ikgj', rot_query, rot_keys, preferred_element_type=...  9.92 us
    another operation x5, other arithmetic  8.21 us
    unnamed x25, local copies, waits for them, and re-layouts  6.46 us
    dot_general x1, matrix products, on_device(): jnp.dot(hidden_piece, w_value, preferred_element_type=jnp.float32)  4.84 us
  transfers between devices with their start and end apart: 2, of which 2 were waited for; matrix products, arithmetic and copies ran while one was open for 12% of the time, Pallas kernels for 0%

commit v1 on v0

v1 whole, which is shorter than its diff:
```python
import functools
import math

import jax
import jax.numpy as jnp
import numpy as np
from jax import lax
from jax.experimental import pallas as pl
from jax.experimental.pallas import tpu as pltpu
from jax.sharding import PartitionSpec as P

HD = 128
GROUP = 8
ROPE_THETA = 500000.0
MESH = pl.DeviceIdType.MESH
UP, DOWN, ACROSS, BACK = 0, 1, 2, 3


def grid_of(cells):
    fast = max(d for d in range(1, math.isqrt(cells) + 1) if cells % d == 0)
    return cells // fast, fast


def rope_tables(rows, slots):
    half = HD // 2
    frequency = (ROPE_THETA ** (-2.0 * np.arange(half) / HD)).astype(np.float32).astype(np.float64)
    frequency = np.concatenate([frequency, frequency])
    row_angle = np.arange(rows)[:, None] * frequency
    place_angle = (np.arange(slots) * rows)[:, None] * frequency
    return [
        np.asarray(t, np.float32)
        for t in (np.cos(row_angle), np.sin(row_angle), np.cos(place_angle), np.sin(place_angle))
    ]


def kernel(
    cells, heads, slots, depth_step,
    hidden, w_key, w_value, queries, order, count, needle, owners, cos_row, sin_row, cos_place, sin_place,
    out,
    own_hidden, far_hidden, key_w, value_w, key_sum, value_sum, q_rows, q_turned,
    kv, k_rot, bias, top, total, mixed,
    hid_sem, far_send, far_recv, kw_sem, vw_sem, q_sem, send_sem, recv_sem,
):
    rows = hidden.shape[0]
    half_depth = hidden.shape[1]
    pieces = half_depth // depth_step
    kv_heads = w_key.shape[1] // HD
    lines, columns = grid_of(cells)
    cell = lax.axis_index("cell")
    head = lax.axis_index("head")
    z = cell // columns
    y = cell % columns

    def at(zz, yy):
        return zz * columns + yy

    def hid_copy(c):
        cols = pl.ds(pl.multiple_of(c * depth_step, depth_step), depth_step)
        return pltpu.make_async_copy(hidden.at[:, cols], own_hidden.at[c], hid_sem.at[c])

    def weight_copy(source, target, sem, c):
        span = pl.ds(pl.multiple_of(c * depth_step, depth_step), depth_step)
        return pltpu.make_async_copy(source.at[span, :], target.at[c], sem.at[c])

    far = [lax.rem(head + step, heads) for step in range(1, heads)]
    for c in range(pieces):
        hid_copy(c).start()
        weight_copy(w_key, key_w, kw_sem, head * pieces + c).start()
        weight_copy(w_value, value_w, vw_sem, head * pieces + c).start()
    for step in range(1, heads):
        back = lax.rem(head + heads - step, heads)
        for c in range(pieces):
            weight_copy(w_key, key_w, kw_sem, back * pieces + c).start()
            weight_copy(w_value, value_w, vw_sem, back * pieces + c).start()
    q_copy = pltpu.make_async_copy(queries, q_rows, q_sem)
    q_copy.start()

    barrier = pltpu.get_barrier_semaphore()
    for other in far:
        pl.semaphore_signal(barrier, inc=1, device_id={"head": other}, device_id_type=MESH)
    exists = {UP: z + 1 < lines, DOWN: z >= 1, ACROSS: y + 1 < columns, BACK: y >= 1}
    target = {UP: cell + columns, DOWN: cell - columns, ACROSS: cell + 1, BACK: cell - 1}
    greeted = jnp.int32(heads - 1)
    for way in (UP, DOWN, ACROSS, BACK):
        greeted = greeted + exists[way].astype(jnp.int32)

        @pl.when(exists[way])
        def _():
            pl.semaphore_signal(barrier, inc=1, device_id={"cell": target[way]}, device_id_type=MESH)

    pl.semaphore_wait(barrier, greeted)

    def far_copy(step, c):
        cols = pl.ds(pl.multiple_of(c * depth_step, depth_step), depth_step)
        return pltpu.make_async_remote_copy(
            src_ref=hidden.at[:, cols], dst_ref=far_hidden.at[step - 1, c],
            send_sem=far_send.at[step - 1, c], recv_sem=far_recv.at[step - 1, c],
            device_id={"head": lax.rem(head + step, heads)}, device_id_type=MESH,
        )

    for step in range(1, heads):
        for c in range(pieces):
            far_copy(step, c).start()

    key_sum[...] = jnp.zeros_like(key_sum)
    value_sum[...] = jnp.zeros_like(value_sum)

    def own_piece(c, carry):
        hid_copy(c).wait()
        w = head * pieces + c
        weight_copy(w_key, key_w, kw_sem, w).wait()
        key_sum[...] += jnp.dot(own_hidden[c], key_w[w], preferred_element_type=jnp.float32)
        weight_copy(w_value, value_w, vw_sem, w).wait()
        value_sum[...] += jnp.dot(own_hidden[c], value_w[w], preferred_element_type=jnp.float32)
        return carry

    lax.fori_loop(0, pieces, own_piece, 0)
    for step in range(1, heads):
        back = lax.rem(head + heads - step, heads)

        def far_piece(c, carry):
            w = back * pieces + c
            far_copy(step, c).wait_recv()
            weight_copy(w_key, key_w, kw_sem, w).wait()
            key_sum[...] += jnp.dot(far_hidden[step - 1, c], key_w[w], preferred_element_type=jnp.float32)
            weight_copy(w_value, value_w, vw_sem, w).wait()
            value_sum[...] += jnp.dot(far_hidden[step - 1, c], value_w[w], preferred_element_type=jnp.float32)
            return carry

        lax.fori_loop(0, pieces, far_piece, 0)

    def shard_copy(way, part, source):
        return pltpu.make_async_remote_copy(
            src_ref=kv.at[part, source], dst_ref=kv.at[part, source],
            send_sem=send_sem.at[way, part, source], recv_sem=recv_sem.at[part, source],
            device_id={"cell": target[way]}, device_id_type=MESH,
        )

    def send(way, part, source, allowed, ending=False):
        @pl.when(allowed)
        def _():
            copy = shard_copy(way, part, source)
            copy.wait_send() if ending else copy.start()

    def arrived(part, source):
        pltpu.make_async_remote_copy(
            src_ref=kv.at[part, source], dst_ref=kv.at[part, source],
            send_sem=send_sem.at[UP, part, source], recv_sem=recv_sem.at[part, source],
            device_id={"cell": lax.rem(cell + 1, cells)}, device_id_type=MESH,
        ).wait_recv()

    kv[0, cell] = key_sum[...].astype(jnp.bfloat16)
    for way in (UP, DOWN, ACROSS, BACK):
        send(way, 0, cell, exists[way])
    kv[1, cell] = value_sum[...].T.astype(jnp.bfloat16)
    for way in (UP, DOWN, ACROSS, BACK):
        send(way, 1, cell, exists[way])

    lane = lax.broadcasted_iota(jnp.int32, (rows, HD), 1)

    def turn_tables(place):
        cos_p = cos_place[pl.ds(place, 1), :]
        sin_p = sin_place[pl.ds(place, 1), :]
        cosine = cos_p * cos_row[...] - sin_p * sin_row[...]
        sine = sin_p * cos_row[...] + cos_p * sin_row[...]
        return cosine, jnp.where(lane < HD // 2, -sine, sine)

    def turned(values, cosine, sine):
        return values * cosine + pltpu.roll(values, HD // 2, 1) * sine

    needle_slot = needle[0]
    used = count[0]
    needle_place = jnp.int32(0)
    for s in range(slots):
        needle_place += jnp.where(needle_slot == s, order[0, s], 0)

    q_copy.wait()
    q_cos, q_sin = turn_tables(needle_place)

    def turn_query(h, carry):
        cols = pl.ds(pl.multiple_of(h * HD, HD), HD)
        row = turned(q_rows[:, cols].astype(jnp.float32), q_cos, q_sin)
        q_turned[h] = row.T.astype(jnp.bfloat16)
        top[h] = jnp.full(top.shape[1:], -1e30, jnp.float32)
        total[h] = jnp.zeros(total.shape[1:], jnp.float32)
        mixed[h] = jnp.zeros(mixed.shape[1:], jnp.float32)
        return carry

    lax.fori_loop(0, kv_heads * GROUP, turn_query, 0)
    exponent = math.log2(math.e) / math.sqrt(HD)

    def attend(source, slot, place):
        offset = jnp.where(
            slot == needle_slot, 0,
            jnp.where((slot >= 0) & (slot < used) & (place < needle_place), rows, -rows),
        )
        cosine, sine = turn_tables(place)
        for k in range(kv_heads):
            block = kv[0, source, :, k * HD:(k + 1) * HD].astype(jnp.float32)
            k_rot[k] = turned(block, cosine, sine).astype(jnp.bfloat16)
        ahead = lax.broadcasted_iota(jnp.int32, (rows, rows), 0) - lax.broadcasted_iota(
            jnp.int32, (rows, rows), 1
        )
        bias[...] = jnp.where(ahead <= offset, 0.0, -jnp.inf)
        for k in range(kv_heads):
            def one_head(g, carry):
                h = k * GROUP + g
                scores = jnp.dot(k_rot[k], q_turned[h], preferred_element_type=jnp.float32) + bias[...]
                before = top[h]
                now = jnp.maximum(before, jnp.max(scores, axis=0, keepdims=True))
                fade = jnp.exp2((before - now) * exponent)
                weights = jnp.exp2((scores - now) * exponent)
                top[h] = now
                total[h] = total[h] * fade + jnp.sum(weights, axis=0, keepdims=True)
                mixed[h] = mixed[h] * fade + jnp.dot(
                    kv[1, source, k * HD:(k + 1) * HD, :], weights.astype(jnp.bfloat16),
                    preferred_element_type=jnp.float32,
                )
                return carry

            lax.fori_loop(0, GROUP, one_head, 0, unroll=4)

    def slot_of(source):
        slot, place = jnp.int32(-1), jnp.int32(0)
        for s in range(slots):
            here = owners[s // 2, s % 2] == source
            slot = jnp.where(here, s, slot)
            place = jnp.where(here, order[0, s], place)
        return slot, place

    def line_round(distance, divert, ending=False):
        for part in (0, 1):
            for way, zz in ((DOWN, z + distance), (UP, z - distance)):
                here = (zz >= 0) & (zz < lines)
                source = at(jnp.clip(zz, 0, lines - 1), y)

                if not ending:
                    @pl.when(here)
                    def _():
                        arrived(part, source)

                send(way, part, source, here & exists[way], ending)
                if divert:
                    kept = ((z == 1) & (zz == 0)) | ((z == lines - 2) & (zz == lines - 1))
                    if part == 0:
                        kept = kept | ((z == 0) & (zz == 1)) | ((z == lines - 1) & (zz == lines - 2))
                    here = here & jnp.logical_not(kept)
                send(ACROSS, part, source, here & exists[ACROSS], ending)
                send(BACK, part, source, here & exists[BACK], ending)

    if cells == slots and columns == 2 and lines == 4:
        mirror = at(z, 1 - y)
        edge = (z == 0) | (z == lines - 1)

        def events(r, ending=False):
            line_round(r, True, ending)
            if r == 1:
                for part in (0, 1):
                    if not ending:
                        arrived(part, mirror)
                    send(UP, part, mirror, z == 0, ending)
                    send(DOWN, part, mirror, z == lines - 1, ending)
            if r == 2:
                send(DOWN, 0, mirror, z == 1, ending)
                send(UP, 0, mirror, z == lines - 2, ending)

        flip = z >= lines // 2
        near = jnp.where(flip, lines - 1 - z, z)
        edge_order = (0, 1, 4, 2, 6, 3, 7, 5)
        inner_order = (1, 0, 2, 5, 3, 4, 6, 7)

        def step(n, carry):
            for r, edge_at, inner_at in ((1, 1, 1), (2, 3, 4), (3, 4, 5)):
                @pl.when(n == jnp.where(near == 0, edge_at, inner_at))
                def _():
                    events(r)

            entry = jnp.int32(0)
            for i in range(2 * lines):
                entry = jnp.where(n == i, jnp.where(near == 0, edge_order[i], inner_order[i]), entry)
            mirrored = entry // lines
            zz = entry % lines
            zz = jnp.where(flip, lines - 1 - zz, zz)
            source = at(zz, jnp.where(mirrored == 1, 1 - y, y))

            @pl.when((mirrored == 1) & (zz != z))
            def _():
                arrived(0, source)
                arrived(1, source)

            slot, place = slot_of(source)
            attend(source, slot, place)
            return carry

        lax.fori_loop(0, 2 * lines, step, 0)
        for r in range(1, lines):
            events(r, True)
    else:
        for r in range(1, lines):
            line_round(r, False)
        for r in range(1, lines):
            line_round(r, False, True)

        def column_step(i, carry):
            distance = 1 + i // lines
            zz = i % lines
            for part in (0, 1):
                for way, yy in ((BACK, y + distance), (ACROSS, y - distance)):
                    here = (yy >= 0) & (yy < columns)
                    source = at(zz, jnp.clip(yy, 0, columns - 1))

                    @pl.when(here)
                    def _():
                        arrived(part, source)

                    @pl.when(here & exists[way])
                    def _():
                        shard_copy(way, part, source).start()
            return carry

        lax.fori_loop(0, (columns - 1) * lines, column_step, 0)

        def column_end(i, carry):
            distance = 1 + i // lines
            zz = i % lines
            for part in (0, 1):
                for way, yy in ((BACK, y + distance), (ACROSS, y - distance)):
                    @pl.when((yy >= 0) & (yy < columns) & exists[way])
                    def _():
                        shard_copy(way, part, at(zz, jnp.clip(yy, 0, columns - 1))).wait_send()
            return carry

        lax.fori_loop(0, (columns - 1) * lines, column_end, 0)

        def slot_step(s, carry):
            attend(owners[s // 2, s % 2], s, order[0, s])
            return carry

        lax.fori_loop(0, slots, slot_step, 0)

    def finish(h, carry):
        cols = pl.ds(pl.multiple_of(h * HD, HD), HD)
        out[:, cols] = (mixed[h] / total[h]).T.astype(jnp.bfloat16)
        return carry

    lax.fori_loop(0, kv_heads * GROUP, finish, 0)

    for step in range(1, heads):
        for c in range(pieces):
            far_copy(step, c).wait_send()
    for part in (0, 1):
        for way in (UP, DOWN, ACROSS, BACK):
            send(way, part, cell, exists[way], True)


def solution(mesh):
    cells, heads = mesh.shape["cell"], mesh.shape["head"]

    def on_device(hidden, w_key, w_value, queries, span_order, span_count, needle, owners):
        rows, half_depth = hidden.shape
        kv_columns = w_key.shape[1]
        kv_heads = kv_columns // HD
        q_heads = kv_heads * GROUP
        slots = span_order.shape[1]
        depth_step = 1024
        pieces = half_depth // depth_step
        tables = [jnp.asarray(t) for t in rope_tables(rows, slots)]
        anywhere = pl.BlockSpec(memory_space=pl.ANY)
        smem = pl.BlockSpec(memory_space=pltpu.SMEM)
        vmem = pl.BlockSpec(memory_space=pltpu.VMEM)
        dma = pltpu.SemaphoreType.DMA
        f32, bf16 = jnp.float32, jnp.bfloat16
        return pl.pallas_call(
            functools.partial(kernel, cells, heads, slots, depth_step),
            out_shape=jax.ShapeDtypeStruct((rows, q_heads * HD), bf16),
            in_specs=[anywhere] * 4 + [smem] * 4 + [vmem] * 4,
            out_specs=vmem,
            scratch_shapes=[
                pltpu.VMEM((pieces, rows, depth_step), bf16),
                pltpu.VMEM((heads - 1, pieces, rows, depth_step), bf16),
                pltpu.VMEM((heads * pieces, depth_step, kv_columns), bf16),
                pltpu.VMEM((heads * pieces, depth_step, kv_columns), bf16),
                pltpu.VMEM((rows, kv_columns), f32),
                pltpu.VMEM((rows, kv_columns), f32),
                pltpu.VMEM((rows, q_heads * HD), bf16),
                pltpu.VMEM((q_heads, HD, rows), bf16),
                pltpu.VMEM((2, cells, rows, kv_columns), bf16),
                pltpu.VMEM((kv_heads, rows, HD), bf16),
                pltpu.VMEM((rows, rows), f32),
                pltpu.VMEM((q_heads, 1, rows), f32),
                pltpu.VMEM((q_heads, 1, rows), f32),
                pltpu.VMEM((q_heads, HD, rows), f32),
                dma((pieces,)),
                dma((heads - 1, pieces)),
                dma((heads - 1, pieces)),
                dma((heads * pieces,)),
                dma((heads * pieces,)),
                dma,
                dma((4, 2, cells)),
                dma((2, cells)),
            ],
            compiler_params=pltpu.CompilerParams(
                collective_id=0, has_side_effects=True, vmem_limit_bytes=56 * 2**20
            ),
            name="span_attention",
        )(hidden, w_key, w_value, queries, span_order, span_count, needle, owners, *tables)

    in_specs = (
        P(("sweep", "cell"), "head"),
        P(None, "head"),
        P(None, "head"),
        P(("sweep", "cell"), "head"),
        P(("sweep", "cell"), None),
        P(("sweep", "cell")),
        P(("sweep", "cell")),
        P("sweep", None),
    )
    return jax.shard_map(
        on_device, mesh=mesh, in_specs=in_specs, out_specs=P(("sweep", "cell"), "head"), check_vma=False
    )
```

time: 159 us -> 73.4 us (0.46)
  Pallas kernels: 0 us -> 68.2 us
  waiting for transfers between devices: 47.9 us -> 0 us
  matrix products: 31.3 us -> 0 us
  local copies, waits for them, and re-layouts: 34.8 us -> 3.64 us
  other arithmetic: 28.9 us -> 0 us
  between operations: 15.8 us -> 1.31 us
    pallas_call x0 -> x1, Pallas kernels: none -> 68.2 us  [on_device(): pl.pallas_call(functools.partial(kernel, cells, heads, slots, depth_step)...]
    all_gather x2 -> x0, waiting for transfers between devices: 47.1 us -> none  [the longest x1 43 us: on_device(): every_span = lax.all_gather(own_span[None], 'cell', axis=0, tiled=True)]
    dot_general x10 -> x0, matrix products: 31.3 us -> none  [the longest x4 15.3 us: on_device(): jnp.einsum('ikgj,jkd->ikgd', weights.astype(jnp.bfloat16), pair_values, p...]
    gather x8 -> x0, local copies, waits for them, and re-layouts: 12.8 us -> none  [the longest x4 10.3 us: on_device(): pair_kv = every_span[owners[round_index]]]
    reduce_sum x4 -> x0, other arithmetic: 10.5 us -> none  [on_device(): attend_weight_sum = attend_weight_sum * rescale + jnp.sum(weights, axis=-1)]
    another operation x6 -> x0, other arithmetic: 8.94 us -> none
    another operation x12 -> x0, local copies, waits for them, and re-layouts: 7.87 us -> none
    convert_element_type x4 -> x0, local copies, waits for them, and re-layouts: 3.43 us -> none  [on_device(): pair_kv[:, 0].reshape(2, span_rows, local_heads, HD).astype(jnp.float32)]
  transfers between devices with their start and end apart: 2 -> 0, of which waited for: 2 -> 0; matrix products, arithmetic and copies ran while one was open for 12% -> 0% of each run, Pallas kernels for 0% -> 0%
where the time goes in v1:
time: 73.4 us; the launch traced here: 73.2 us
  Pallas kernels  68.2 us (93%)
  local copies, waits for them, and re-layouts  3.64 us (5%)
  between operations  1.31 us (2%)
    pallas_call x1, Pallas kernels, on_device(): pl.pallas_call(functools.partial(kernel, cells, heads, slots, depth_step)...  68.2 us
    unnamed x2, local copies, waits for them, and re-layouts  3.64 us

profile of v1, /device:TPU:0, one launch (start us, length us, event | category | flops | bytes accessed | tf_op | source)
XLA Modules:
  0.0 73.2 jit_solution(12459014157750206624)
XLA Ops:
  1.3 1.3 %copy.13.owners = s32[4,2]{1,0:T(4,128)} copy(s32[4,2]{0,1:T(2,128)} %param.19) | data formatting | bytes 64 | tf_op args[7]
  2.6 68.2 %span_attention.1 = bf16[256,2048]{1,0:T(8,128)(2,1)} custom-call(bf16[256,4096]{1,0:T(8,128)(2,1)} %hidden.1, bf16[8192,256]{1,0:T(8,128)(2,1)} %w_key.1, bf16[8192,256]{1,0:T(8,128)(2,1)} %w_value.1, bf16[256,2048]{1,0:T(8,128)(2,1)} %queries.1, s32[1,8]{1,0:T(1,128)} %order.1, s32[1]{0:T(128)S(6)} %copy.15.count, s32[1]{0:T(128)S(6)} %copy.16.needle, ...), custom_call_target="tpu_custom_call" | custom-call | tf_op jit(solution)/shard_map/span_attention/pallas_call | solution.py:373
  70.9 2.3 %copy.17 = bf16[256,2048]{1,0:T(8,128)(2,1)} copy(bf16[256,2048]{1,0:T(8,128)(2,1)} %span_attention.1) | data formatting | bytes 2097152

commit v2 on v1

--- a/solution.py
+++ b/solution.py
@@ -14,6 +14,7 @@
 ROPE_THETA = 500000.0
 MESH = pl.DeviceIdType.MESH
 UP, DOWN, ACROSS, BACK = 0, 1, 2, 3
+AHEAD, BEHIND = 2, 1
 
 
 def grid_of(cells):
@@ -202,23 +203,34 @@
             jnp.int32, (rows, rows), 1
         )
         bias[...] = jnp.where(ahead <= offset, 0.0, -jnp.inf)
-        for k in range(kv_heads):
-            def one_head(g, carry):
-                h = k * GROUP + g
-                scores = jnp.dot(k_rot[k], q_turned[h], preferred_element_type=jnp.float32) + bias[...]
-                before = top[h]
-                now = jnp.maximum(before, jnp.max(scores, axis=0, keepdims=True))
-                fade = jnp.exp2((before - now) * exponent)
-                weights = jnp.exp2((scores - now) * exponent)
-                top[h] = now
-                total[h] = total[h] * fade + jnp.sum(weights, axis=0, keepdims=True)
-                mixed[h] = mixed[h] * fade + jnp.dot(
-                    kv[1, source, k * HD:(k + 1) * HD, :], weights.astype(jnp.bfloat16),
-                    preferred_element_type=jnp.float32,
-                )
-                return carry
-
-            lax.fori_loop(0, GROUP, one_head, 0, unroll=4)
+        def score(h):
+            return jnp.dot(k_rot[h // GROUP], q_turned[h], preferred_element_type=jnp.float32) + bias[...]
+
+        def mix(h, fade, weights):
+            k = h // GROUP
+            mixed[h] = mixed[h] * fade + jnp.dot(
+                kv[1, source, k * HD:(k + 1) * HD, :], weights, preferred_element_type=jnp.float32
+            )
+
+        q_heads = kv_heads * GROUP
+        olds = [(top[h], total[h]) for h in range(q_heads)]
+        news, scored, pending = [], [score(h) for h in range(AHEAD)], []
+        for h in range(q_heads):
+            if h + AHEAD < q_heads:
+                scored.append(score(h + AHEAD))
+            scores = scored[h]
+            before, summed = olds[h]
+            now = jnp.maximum(before, jnp.max(scores, axis=0, keepdims=True))
+            fade = jnp.exp2((before - now) * exponent)
+            weights = jnp.exp2((scores - now) * exponent)
+            news.append((now, summed * fade + jnp.sum(weights, axis=0, keepdims=True)))
+            pending.append((h, fade, weights.astype(jnp.bfloat16)))
+            if len(pending) > BEHIND:
+                mix(*pending.pop(0))
+        for item in pending:
+            mix(*item)
+        for h in range(q_heads):
+            top[h], total[h] = news[h]
 
     def slot_of(source):
         slot, place = jnp.int32(-1), jnp.int32(0)
@@ -362,7 +374,7 @@
         kv_heads = kv_columns // HD
         q_heads = kv_heads * GROUP
         slots = span_order.shape[1]
-        depth_step = 1024
+        depth_step = 2048
         pieces = half_depth // depth_step
         tables = [jnp.asarray(t) for t in rope_tables(rows, slots)]
         anywhere = pl.BlockSpec(memory_space=pl.ANY)

time: 73.4 us -> 49.7 us (0.68)
  Pallas kernels: 68.2 us -> 44.5 us
    pallas_call x1, Pallas kernels: 68.2 us -> 44.5 us  [on_device(): pl.pallas_call(functools.partial(kernel, cells, heads, slots, depth_step)...]
where the time goes in v2:
time: 49.7 us; the launch traced here: 49.5 us
  Pallas kernels  44.5 us (90%)
  local copies, waits for them, and re-layouts  3.64 us (7%)
  between operations  1.31 us (3%)
    pallas_call x1, Pallas kernels, on_device(): pl.pallas_call(functools.partial(kernel, cells, heads, slots, depth_step)...  44.5 us
    unnamed x2, local copies, waits for them, and re-layouts  3.64 us

profile of v2, /device:TPU:0, one launch (start us, length us, event | category | flops | bytes accessed | tf_op | source)
XLA Modules:
  0.0 49.5 jit_solution(3782912364117371291)
XLA Ops:
  1.3 1.3 %copy.13.owners = s32[4,2]{1,0:T(4,128)} copy(s32[4,2]{0,1:T(2,128)} %param.19) | data formatting | bytes 64 | tf_op args[7]
  2.6 44.5 %span_attention.1 = bf16[256,2048]{1,0:T(8,128)(2,1)} custom-call(bf16[256,4096]{1,0:T(8,128)(2,1)} %hidden.1, bf16[8192,256]{1,0:T(8,128)(2,1)} %w_key.1, bf16[8192,256]{1,0:T(8,128)(2,1)} %w_value.1, bf16[256,2048]{1,0:T(8,128)(2,1)} %queries.1, s32[1,8]{1,0:T(1,128)} %order.1, s32[1]{0:T(128)S(6)} %copy.15.count, s32[1]{0:T(128)S(6)} %copy.16.needle, ...), custom_call_target="tpu_custom_call" | custom-call | tf_op jit(solution)/shard_map/span_attention/pallas_call | solution.py:385
  47.2 2.3 %copy.17 = bf16[256,2048]{1,0:T(8,128)(2,1)} copy(bf16[256,2048]{1,0:T(8,128)(2,1)} %span_attention.1) | data formatting | bytes 2097152
